TPU v7x, 32 devices: a whole 2x2x4 slice. The times are simulated.
32 devices in a mesh: row: 16 (over z, y, x), col: 2 (over core).
Axes of the slice: x: 2, y: 2, z: 4, core: 2. Of those that a mesh axis runs over, the one named last changes fastest.
Arguments:
- panel: float32 [12288, 512], P(('row', 'col')), may hold values from -600 to 600
- trailing: float32 [12288, 1024], P('row', 'col'), may hold values from -6 to 6
Outputs:
- r_factor: float32 [512, 512], replicated
- residual: float32 [12288, 1024], P('row', 'col')
All inputs are finite; a program needn't handle non-finite values.
Results may differ from a plain program's by a relative error of at most 0.0003.
Values sent between devices are 32-bit elements; how exact they have to be, the bound alone decides.
A program may use at most 64 MiB of HBM per device.

v0:
```python
import functools, math
import jax
import jax.numpy as jnp
from jax import lax
from jax.experimental import pallas as pl
from jax.experimental.pallas import tpu as pltpu
from jax.sharding import PartitionSpec as P

HI = lax.Precision.HIGHEST
NB = 128
G = 16
TN = (((0,), (0,)), ((), ()))


def split3(x):
    h = x.astype(jnp.bfloat16).astype(jnp.float32)
    rest = x - h
    m = rest.astype(jnp.bfloat16).astype(jnp.float32)
    return h, m, rest - m


def factor_block(d_ref):
    rows = lax.broadcasted_iota(jnp.int32, (G, NB), 0)
    for r0 in range(0, NB, G):
        left, right = d_ref[r0:r0 + G, :NB], d_ref[r0:r0 + G, NB:]
        cols = [jnp.broadcast_to(left[:, r0 + j:r0 + j + 1], (G, NB)) for j in range(G)]
        scale = jnp.zeros((G, NB), jnp.float32)
        for j in range(G):
            pivot = jnp.broadcast_to(cols[j][j:j + 1], (G, NB))
            inv = 1.0 / pivot
            scale = jnp.where(rows == j, lax.rsqrt(pivot), scale)
            below = jnp.where(rows > j, cols[j] * inv, 0.0)
            for c in range(j + 1, G):
                cols[c] = cols[c] - below * cols[c][j:j + 1]
            left = left - below * left[j:j + 1]
            right = right - below * right[j:j + 1]
        left, right = left * scale, right * scale
        d_ref[r0:r0 + G, :NB] = left
        d_ref[r0:r0 + G, NB:] = right
        if r0 + G < NB:
            both = jnp.concatenate([left, right], axis=1)
            h, m, l = split3(both)
            a = jnp.concatenate([v[:, :NB] for v in (h, h, m, m, h, l)], axis=0)
            b = jnp.concatenate([h, m, h, m, l, h], axis=0).astype(jnp.bfloat16)
            at = a.T.astype(jnp.bfloat16)
            upd = jnp.dot(at, b, preferred_element_type=jnp.float32)
            d_ref[r0 + G:, :] = d_ref[r0 + G:, :] - upd[r0 + G:, :]


def factor(m_ref, d_ref, size, between):
    eye = (lax.broadcasted_iota(jnp.int32, (NB, NB), 0) == lax.broadcasted_iota(jnp.int32, (NB, NB), 1)).astype(jnp.float32)
    steps = size // NB

    def step(k, _):
        at = pl.ds(pl.multiple_of(k * NB, NB), NB)
        d_ref[:, :NB] = m_ref[at, at]
        d_ref[:, NB:] = eye
        factor_block(d_ref)
        m_ref[at, :] = jnp.dot(d_ref[:, NB:], m_ref[at, :], precision=HI, preferred_element_type=jnp.float32)

        def below(i, _):
            to = pl.ds(pl.multiple_of(i * NB, NB), NB)
            m_ref[to, :] = m_ref[to, :] - lax.dot_general(m_ref[at, to], m_ref[at, :], TN, precision=HI, preferred_element_type=jnp.float32)
            return 0

        lax.fori_loop(k + 1, steps, below, 0)
        between(k)
        return 0

    lax.fori_loop(0, steps, step, 0)


class Sum:
    def __init__(self, n1, n2, part, got1, mid, got2, full, send, recv):
        self.n1, self.n2 = n1, n2
        self.part, self.got1, self.mid, self.got2, self.full = part, got1, mid, got2, full
        self.send, self.recv = send, recv
        me = lax.axis_index("row")
        self.outer, self.inner = me // n1, lax.rem(me, n1)
        self.col = lax.axis_index("col")

    def copies(self, phase):
        n1, n2, inner, outer = self.n1, self.n2, self.inner, self.outer
        first = (0, n1 - 1, n1 + n2 - 2, n1 + 2 * n2 - 3)[phase]
        out = []
        for k in range(1, n1 if phase in (0, 3) else n2):
            if phase in (0, 3):
                peer = lax.rem(inner + k, n1)
                target = outer * n1 + peer
            else:
                peer = lax.rem(outer + k, n2)
                target = peer * n1 + inner
            if phase == 0:
                src, dst = self.part.at[peer], self.got1.at[k - 1]
            elif phase == 1:
                src, dst = self.mid.at[peer], self.got2.at[k - 1]
            elif phase == 2:
                src = dst = self.full.at[inner, outer]
            else:
                src = dst = self.full.at[inner]
            out.append(pltpu.make_async_remote_copy(
                src_ref=src, dst_ref=dst, send_sem=self.send.at[first + k - 1],
                recv_sem=self.recv.at[first + k - 1], device_id=(target, self.col),
                device_id_type=pl.DeviceIdType.MESH))
        return out

    def start(self, phase):
        for copy in self.copies(phase):
            copy.start()

    def finish(self, phase):
        if phase == 0:
            total = self.part[self.inner]
            for k, copy in enumerate(self.copies(0)):
                copy.wait_recv()
                total = total + self.got1[k]
            self.mid[...] = total
        elif phase == 1:
            total = self.mid[self.outer]
            for k, copy in enumerate(self.copies(1)):
                copy.wait_recv()
                total = total + self.got2[k]
            self.full[self.inner, self.outer] = total
        else:
            for copy in self.copies(phase):
                copy.wait_recv()

    def drain(self):
        for phase in range(4):
            for copy in self.copies(phase):
                copy.wait_send()


def kernel(n, m, n1, split, total_rows, panel_ref, trailing_ref, r_ref, out_ref, block, gpart, ggot1, gmid, ggot2, gfull,
           cpart, cgot1, cmid, cgot2, cfull, m_ref, d_ref, gsend, grecv, csend, crecv, bsend, brecv, esend, erecv):
    n2 = n // n1
    size = panel_ref.shape[1]
    own = panel_ref.shape[0]
    row, col = lax.axis_index("row"), lax.axis_index("col")
    outer, inner = row // n1, lax.rem(row, n1)
    MESH = pl.DeviceIdType.MESH
    barrier = pltpu.get_barrier_semaphore()
    for k in range(1, m):
        pl.semaphore_signal(barrier, inc=1, device_id=(row, lax.rem(col + k, m)), device_id_type=MESH)
    for k in range(1, n1):
        pl.semaphore_signal(barrier, inc=1, device_id=(outer * n1 + lax.rem(inner + k, n1), col), device_id_type=MESH)
    for k in range(1, n2):
        pl.semaphore_signal(barrier, inc=1, device_id=(lax.rem(outer + k, n2) * n1 + inner, col), device_id_type=MESH)
    pl.semaphore_wait(barrier, m + n1 + n2 - 3)

    def spread(src, dst, send, recv):
        return [pltpu.make_async_remote_copy(
            src_ref=src, dst_ref=dst, send_sem=send.at[k - 1], recv_sem=recv.at[k - 1],
            device_id=(row, lax.rem(col + k, m)), device_id_type=MESH) for k in range(1, m)]

    gather = spread(panel_ref, block.at[col], bsend, brecv)
    for copy in gather:
        copy.start()
    block[col] = panel_ref[...]

    def tn(a, b):
        return lax.dot_general(a, b, TN, precision=HI, preferred_element_type=jnp.float32)

    half = size // split
    cols = pl.ds(pl.multiple_of(col * half, half), half) if split > 1 else pl.ds(0, size)
    total = tn(panel_ref[:, cols], panel_ref[...])
    for k, copy in enumerate(gather):
        copy.wait_recv()
        other = lax.rem(col + m - k - 1, m)
        total = total + tn(block[other, :, cols], block[other])
    gpart[...] = total.reshape(gpart.shape)
    gsum = Sum(n1, n2, gpart, ggot1, gmid, ggot2, gfull.at[col if split > 1 else 0], gsend, grecv)
    csum = Sum(n1, n2, cpart, cgot1, cmid, cgot2, cfull, csend, crecv)
    gsum.start(0)
    cross = tn(block[0], trailing_ref[:own, :])
    for k in range(1, m):
        cross = cross + tn(block[k], trailing_ref[k * own:(k + 1) * own, :])
    cpart[...] = cross.reshape(cpart.shape)
    for phase in range(4):
        gsum.finish(phase)
        if phase < 3:
            gsum.start(phase + 1)
    share = spread(gsum.full, gsum.full, esend, erecv) if split > 1 else []
    for copy in share:
        copy.start()
    csum.start(0)
    for copy in share:
        copy.wait_recv()
    m_ref[:, :size] = gfull[...].reshape(size, size)
    r = lax.broadcasted_iota(jnp.int32, (size, size), 0)
    c = lax.broadcasted_iota(jnp.int32, (size, size), 1)
    m_ref[:, size:] = (r == c).astype(jnp.float32)

    steps = size // NB

    def between(k):
        for phase in range(4):
            @pl.when(k == phase * (steps - 1) // 3)
            def _():
                csum.finish(phase)
                if phase < 3:
                    csum.start(phase + 1)

    factor(m_ref, d_ref, size, between)
    r = lax.broadcasted_iota(jnp.int32, (size, size), 0)
    c = lax.broadcasted_iota(jnp.int32, (size, size), 1)
    r_ref[...] = jnp.where(c >= r, m_ref[:, :size] * (1.0 / math.sqrt(total_rows)), 0.0)
    w = m_ref[:, size:]
    coupling = jnp.dot(w, cfull[...].reshape(size, cfull.shape[-1]), precision=HI, preferred_element_type=jnp.float32)
    combined = tn(w, coupling)
    for k in range(m):
        at = slice(k * own, (k + 1) * own)
        out_ref[at, :] = trailing_ref[at, :] - jnp.dot(block[k], combined, precision=HI, preferred_element_type=jnp.float32)
    gsum.drain()
    csum.drain()
    for copy in gather + share:
        copy.wait_send()


def per_device(panel, trailing):
    n, m = lax.axis_size("row"), lax.axis_size("col")
    own, size = panel.shape
    width = trailing.shape[1]
    n1 = 4 if n % 4 == 0 else n
    n2 = n // n1
    split = m if size % (8 * n * m) == 0 and (size // m) % 128 == 0 else 1
    f32 = jnp.float32

    def buffers(rows, cols, copies):
        s = rows // n
        lead = (copies,) if copies else ()
        return [pltpu.VMEM((n1, n2, s, cols), f32), pltpu.VMEM((max(n1 - 1, 1), n2, s, cols), f32),
                pltpu.VMEM((n2, s, cols), f32), pltpu.VMEM((max(n2 - 1, 1), s, cols), f32),
                pltpu.VMEM(lead + (n1, n2, s, cols), f32)]

    dma = pltpu.SemaphoreType.DMA
    hops = 2 * (n1 + n2 - 2)
    vmem = pl.BlockSpec(memory_space=pltpu.VMEM)
    return pl.pallas_call(
        functools.partial(kernel, n, m, n1, split, own * n * m),
        out_shape=(jax.ShapeDtypeStruct((size, size), f32), jax.ShapeDtypeStruct(trailing.shape, f32)),
        in_specs=[vmem] * 2,
        out_specs=[vmem] * 2,
        scratch_shapes=[pltpu.VMEM((m, own, size), f32)] + buffers(size // split, size, split) + buffers(size, width, 0)
        + [pltpu.VMEM((size, 2 * size), f32), pltpu.VMEM((NB, 2 * NB), f32)]
        + [dma((hops,))] * 4 + [dma((max(m - 1, 1),))] * 4,
        compiler_params=pltpu.CompilerParams(collective_id=0, has_side_effects=True, vmem_limit_bytes=56 << 20),
    )(panel, trailing)


def solution(mesh):
    return jax.shard_map(
        per_device, mesh=mesh, in_specs=(P(("row", "col"), None), P("row", "col")),
        out_specs=(P(), P("row", "col")), check_vma=False)
```

profile of v0, /device:TPU:26, one launch (start us, length us, event | category | flops | bytes accessed | tf_op | source)
XLA Modules:
  0.0 81.4 jit_solution(2249559325637098019)
XLA Ops:
  0.6 77.2 %shard_map.41 = (f32[512,512]{1,0:T(8,128)}, f32[768,512]{1,0:T(8,128)}) custom-call(f32[384,512]{1,0:T(8,128)} %panel_ref.1, f32[768,512]{1,0:T(8,128)} %trailing_ref.1), custom_call_target="tpu_custom_call" | custom-call | tf_op jit(solution)/shard_map/pallas_call | solution.py:239
  77.8 0.0 copy-start
  77.9 2.4 %copy.6 = f32[512,512]{1,0:T(8,128)} copy(f32[512,512]{1,0:T(8,128)} %get-tuple-element.4) | data formatting | bytes 2097152
  80.2 0.0 copy-done
  80.2 1.1 %copy.7 = f32[768,512]{1,0:T(8,128)} copy(f32[768,512]{1,0:T(8,128)S(1)} %copy-done) | data formatting | bytes 3145728
Async XLA Ops:
  77.8 2.4 %copy-start = (f32[768,512]{1,0:T(8,128)S(1)}, f32[768,512]{1,0:T(8,128)}, u32[]{:S(2)}) copy-start(f32[768,512]{1,0:T(8,128)} %get-tuple-element.5) | copy-start | bytes 4718596
where the time goes:
time: 81.6 us; the launch traced here: 81.4 us
  Pallas kernels  77.2 us (95%)
  local copies, waits for them, and re-layouts  3.53 us (4%)
    pallas_call x1, Pallas kernels, per_device(): pl.pallas_call(functools.partial(kernel, n, m, n1, split, own * n * m), o...  77.2 us
    unnamed x4, local copies, waits for them, and re-layouts  3.53 us

commit v1 on v0

--- a/solution.py
+++ b/solution.py
@@ -6,10 +6,23 @@
 from jax.experimental.pallas import tpu as pltpu
 from jax.sharding import PartitionSpec as P
 
-HI = lax.Precision.HIGHEST
 NB = 128
 G = 16
 TN = (((0,), (0,)), ((), ()))
+
+
+NN = (((1,), (0,)), ((), ()))
+
+
+def split2(x):
+    h = x.astype(jnp.bfloat16)
+    return h, (x - h.astype(jnp.float32)).astype(jnp.bfloat16)
+
+
+def dot3(a, b, dims=NN):
+    def dot(x, y):
+        return lax.dot_general(x, y, dims, preferred_element_type=jnp.float32)
+    return dot(a[0], b[0]) + (dot(a[0], b[1]) + dot(a[1], b[0]))
 
 
 def split3(x):
@@ -50,24 +63,25 @@
 def factor(m_ref, d_ref, size, between):
     eye = (lax.broadcasted_iota(jnp.int32, (NB, NB), 0) == lax.broadcasted_iota(jnp.int32, (NB, NB), 1)).astype(jnp.float32)
     steps = size // NB
-
-    def step(k, _):
-        at = pl.ds(pl.multiple_of(k * NB, NB), NB)
+    for k in range(steps):
+        at, window = slice(k * NB, (k + 1) * NB), slice(k * NB, (k + 1) * NB + size)
         d_ref[:, :NB] = m_ref[at, at]
         d_ref[:, NB:] = eye
         factor_block(d_ref)
-        m_ref[at, :] = jnp.dot(d_ref[:, NB:], m_ref[at, :], precision=HI, preferred_element_type=jnp.float32)
-
-        def below(i, _):
-            to = pl.ds(pl.multiple_of(i * NB, NB), NB)
-            m_ref[to, :] = m_ref[to, :] - lax.dot_general(m_ref[at, to], m_ref[at, :], TN, precision=HI, preferred_element_type=jnp.float32)
-            return 0
-
-        lax.fori_loop(k + 1, steps, below, 0)
-        between(k)
-        return 0
-
-    lax.fori_loop(0, steps, step, 0)
+        done = dot3(split2(d_ref[:, NB:]), split2(m_ref[at, window]))
+        m_ref[at, window] = done
+        if k + 1 < steps:
+            done = split2(done)
+            right = tuple(v[:, NB:size - k * NB] for v in done)
+            m_ref[(k + 1) * NB:, window] = m_ref[(k + 1) * NB:, window] - dot3(right, done, TN)
+        between(k + 1)
+
+
+def tiles(steps, split, col):
+    if split == 1:
+        return [(i, j) for i in range(steps) for j in range(i, steps)]
+    first = [(col, col + t) for t in range(steps - col)]
+    return first + [(steps - 1 - col, j) for j in range(steps - 1 - col, steps)]
 
 
 class Sum:
@@ -131,7 +145,7 @@
                 copy.wait_send()
 
 
-def kernel(n, m, n1, split, total_rows, panel_ref, trailing_ref, r_ref, out_ref, block, gpart, ggot1, gmid, ggot2, gfull,
+def kernel(n, m, n1, split, total_rows, panel_ref, trailing_ref, r_ref, out_ref, block, strip, gpart, ggot1, gmid, ggot2, gfull,
            cpart, cgot1, cmid, cgot2, cfull, m_ref, d_ref, gsend, grecv, csend, crecv, bsend, brecv, esend, erecv):
     n2 = n // n1
     size = panel_ref.shape[1]
@@ -158,59 +172,73 @@
         copy.start()
     block[col] = panel_ref[...]
 
-    def tn(a, b):
-        return lax.dot_general(a, b, TN, precision=HI, preferred_element_type=jnp.float32)
-
-    half = size // split
-    cols = pl.ds(pl.multiple_of(col * half, half), half) if split > 1 else pl.ds(0, size)
-    total = tn(panel_ref[:, cols], panel_ref[...])
+    steps = size // NB
+    count = len(tiles(steps, split, 0))
+    m_ref[:, :size] = jnp.zeros((size, size), jnp.float32)
+    r = lax.broadcasted_iota(jnp.int32, (size, size), 0)
+    c = lax.broadcasted_iota(jnp.int32, (size, size), 1)
+    m_ref[:, size:] = (r == c).astype(jnp.float32)
+
+    def cut(x, i):
+        return x[:, pl.ds(pl.multiple_of(i * NB, NB), NB)]
+
+    strips = range(steps) if split == 1 else (col, steps - 1 - col)
+
+    def gram(x):
+        return dot3(split2(jnp.concatenate([cut(x, i) for i in strips], axis=1)), split2(x[...]), TN)
+
+    strip[...] = gram(panel_ref)
     for k, copy in enumerate(gather):
         copy.wait_recv()
-        other = lax.rem(col + m - k - 1, m)
-        total = total + tn(block[other, :, cols], block[other])
-    gpart[...] = total.reshape(gpart.shape)
+        strip[...] = strip[...] + gram(block.at[lax.rem(col + m - k - 1, m)])
+    if split == 1:
+        picked = [strip[i * NB:(i + 1) * NB, j * NB:(j + 1) * NB] for i, j in tiles(steps, 1, 0)]
+    else:
+        picked = []
+        for t in range(count):
+            low = t >= steps - col
+            i, j = jnp.where(low, 1, 0), jnp.where(low, t - 1, col + t)
+            picked.append(strip[pl.ds(pl.multiple_of(i * NB, NB), NB), pl.ds(pl.multiple_of(j * NB, NB), NB)])
+    gpart[...] = jnp.concatenate(picked, axis=0).reshape(gpart.shape)
     gsum = Sum(n1, n2, gpart, ggot1, gmid, ggot2, gfull.at[col if split > 1 else 0], gsend, grecv)
     csum = Sum(n1, n2, cpart, cgot1, cmid, cgot2, cfull, csend, crecv)
     gsum.start(0)
-    cross = tn(block[0], trailing_ref[:own, :])
-    for k in range(1, m):
-        cross = cross + tn(block[k], trailing_ref[k * own:(k + 1) * own, :])
+    cross = jnp.zeros((size, trailing_ref.shape[1]), jnp.float32)
+    for k in range(m):
+        cross = cross + dot3(split2(block[k]), split2(trailing_ref[k * own:(k + 1) * own, :]), TN)
     cpart[...] = cross.reshape(cpart.shape)
     for phase in range(4):
         gsum.finish(phase)
         if phase < 3:
             gsum.start(phase + 1)
+        if phase == 0:
+            csum.start(0)
     share = spread(gsum.full, gsum.full, esend, erecv) if split > 1 else []
     for copy in share:
         copy.start()
-    csum.start(0)
     for copy in share:
         copy.wait_recv()
-    m_ref[:, :size] = gfull[...].reshape(size, size)
-    r = lax.broadcasted_iota(jnp.int32, (size, size), 0)
-    c = lax.broadcasted_iota(jnp.int32, (size, size), 1)
-    m_ref[:, size:] = (r == c).astype(jnp.float32)
-
-    steps = size // NB
+    for k in range(split):
+        flat = gfull[k].reshape(count * NB, NB)
+        for t, (i, j) in enumerate(tiles(steps, split, k)):
+            m_ref[i * NB:(i + 1) * NB, j * NB:(j + 1) * NB] = flat[t * NB:(t + 1) * NB]
 
     def between(k):
         for phase in range(4):
-            @pl.when(k == phase * (steps - 1) // 3)
-            def _():
+            if k == (steps if phase == 3 else phase * steps // 4):
                 csum.finish(phase)
                 if phase < 3:
                     csum.start(phase + 1)
 
+    between(0)
     factor(m_ref, d_ref, size, between)
-    r = lax.broadcasted_iota(jnp.int32, (size, size), 0)
-    c = lax.broadcasted_iota(jnp.int32, (size, size), 1)
     r_ref[...] = jnp.where(c >= r, m_ref[:, :size] * (1.0 / math.sqrt(total_rows)), 0.0)
-    w = m_ref[:, size:]
-    coupling = jnp.dot(w, cfull[...].reshape(size, cfull.shape[-1]), precision=HI, preferred_element_type=jnp.float32)
-    combined = tn(w, coupling)
+    w = split2(m_ref[:, size:])
+    coupling = dot3(w, split2(cfull[...].reshape(size, cfull.shape[-1])))
+    combined = split2(dot3(w, split2(coupling), TN))
     for k in range(m):
         at = slice(k * own, (k + 1) * own)
-        out_ref[at, :] = trailing_ref[at, :] - jnp.dot(block[k], combined, precision=HI, preferred_element_type=jnp.float32)
+        out_ref[at, :] = trailing_ref[at, :] - dot3(split2(block[k]), combined)
     gsum.drain()
     csum.drain()
     for copy in gather + share:
@@ -223,7 +251,9 @@
     width = trailing.shape[1]
     n1 = 4 if n % 4 == 0 else n
     n2 = n // n1
-    split = m if size % (8 * n * m) == 0 and (size // m) % 128 == 0 else 1
+    steps = size // NB
+    split = m if steps == 2 * m and (steps + 1) * NB % (8 * n) == 0 else 1
+    count = len(tiles(steps, split, 0))
     f32 = jnp.float32
 
     def buffers(rows, cols, copies):
@@ -241,7 +271,8 @@
         out_shape=(jax.ShapeDtypeStruct((size, size), f32), jax.ShapeDtypeStruct(trailing.shape, f32)),
         in_specs=[vmem] * 2,
         out_specs=[vmem] * 2,
-        scratch_shapes=[pltpu.VMEM((m, own, size), f32)] + buffers(size // split, size, split) + buffers(size, width, 0)
+        scratch_shapes=[pltpu.VMEM((m, own, size), f32), pltpu.VMEM((size if split == 1 else 2 * NB, size), f32)]
+        + buffers(count * NB, NB, split) + buffers(size, width, 0)
         + [pltpu.VMEM((size, 2 * size), f32), pltpu.VMEM((NB, 2 * NB), f32)]
         + [dma((hops,))] * 4 + [dma((max(m - 1, 1),))] * 4,
         compiler_params=pltpu.CompilerParams(collective_id=0, has_side_effects=True, vmem_limit_bytes=56 << 20),

time: 81.6 us -> 86.6 us (1.061)
  the two profiles are of different devices: /device:TPU:26 before, /device:TPU:0 now
where the time goes in v1:
time: 86.6 us; the launch traced here: 86.4 us
  Pallas kernels  82.2 us (95%)
  local copies, waits for them, and re-layouts  3.53 us (4%)
    pallas_call x1, Pallas kernels, per_device(): pl.pallas_call(functools.partial(kernel, n, m, n1, split, own * n * m), o...  82.2 us
    unnamed x4, local copies, waits for them, and re-layouts  3.53 us

profile of v1, /device:TPU:0, one launch (start us, length us, event | category | flops | bytes accessed | tf_op | source)
XLA Modules:
  0.0 86.4 jit_solution(13461514089958700195)
XLA Ops:
  0.6 82.2 %shard_map.41 = (f32[512,512]{1,0:T(8,128)}, f32[768,512]{1,0:T(8,128)}) custom-call(f32[384,512]{1,0:T(8,128)} %panel_ref.1, f32[768,512]{1,0:T(8,128)} %trailing_ref.1), custom_call_target="tpu_custom_call" | custom-call | tf_op jit(solution)/shard_map/pallas_call | solution.py:269
  82.9 0.0 copy-start
  82.9 2.4 %copy.6 = f32[512,512]{1,0:T(8,128)} copy(f32[512,512]{1,0:T(8,128)} %get-tuple-element.4) | data formatting | bytes 2097152
  85.2 0.0 copy-done
  85.2 1.1 %copy.7 = f32[768,512]{1,0:T(8,128)} copy(f32[768,512]{1,0:T(8,128)S(1)} %copy-done) | data formatting | bytes 3145728
Async XLA Ops:
  82.9 2.4 %copy-start = (f32[768,512]{1,0:T(8,128)S(1)}, f32[768,512]{1,0:T(8,128)}, u32[]{:S(2)}) copy-start(f32[768,512]{1,0:T(8,128)} %get-tuple-element.5) | copy-start | bytes 4718596

commit v2 on v1

--- a/solution.py
+++ b/solution.py
@@ -153,6 +153,7 @@
     row, col = lax.axis_index("row"), lax.axis_index("col")
     outer, inner = row // n1, lax.rem(row, n1)
     MESH = pl.DeviceIdType.MESH
+    here = pl.when(row >= 0)
     barrier = pltpu.get_barrier_semaphore()
     for k in range(1, m):
         pl.semaphore_signal(barrier, inc=1, device_id=(row, lax.rem(col + k, m)), device_id_type=MESH)
@@ -168,8 +169,7 @@
             device_id=(row, lax.rem(col + k, m)), device_id_type=MESH) for k in range(1, m)]
 
     gather = spread(panel_ref, block.at[col], bsend, brecv)
-    for copy in gather:
-        copy.start()
+    here(lambda: [copy.start() for copy in gather] and None)
     block[col] = panel_ref[...]
 
     steps = size // NB
@@ -202,17 +202,18 @@
     gpart[...] = jnp.concatenate(picked, axis=0).reshape(gpart.shape)
     gsum = Sum(n1, n2, gpart, ggot1, gmid, ggot2, gfull.at[col if split > 1 else 0], gsend, grecv)
     csum = Sum(n1, n2, cpart, cgot1, cmid, cgot2, cfull, csend, crecv)
-    gsum.start(0)
+    here(lambda: gsum.start(0))
     cross = jnp.zeros((size, trailing_ref.shape[1]), jnp.float32)
     for k in range(m):
         cross = cross + dot3(split2(block[k]), split2(trailing_ref[k * own:(k + 1) * own, :]), TN)
     cpart[...] = cross.reshape(cpart.shape)
+    here(lambda: csum.start(0))
     for phase in range(4):
-        gsum.finish(phase)
-        if phase < 3:
-            gsum.start(phase + 1)
-        if phase == 0:
-            csum.start(0)
+        @here
+        def _():
+            gsum.finish(phase)
+            if phase < 3:
+                gsum.start(phase + 1)
     share = spread(gsum.full, gsum.full, esend, erecv) if split > 1 else []
     for copy in share:
         copy.start()
@@ -226,9 +227,11 @@
     def between(k):
         for phase in range(4):
             if k == (steps if phase == 3 else phase * steps // 4):
-                csum.finish(phase)
-                if phase < 3:
-                    csum.start(phase + 1)
+                @here
+                def _():
+                    csum.finish(phase)
+                    if phase < 3:
+                        csum.start(phase + 1)
 
     between(0)
     factor(m_ref, d_ref, size, between)

time: 86.6 us -> 66.3 us (0.77)
  Pallas kernels: 82.2 us -> 62 us
    pallas_call x1, Pallas kernels: 82.2 us -> 62 us  [per_device(): pl.pallas_call(functools.partial(kernel, n, m, n1, split, own * n * m), o...]
where the time goes in v2:
time: 66.3 us; the launch traced here: 66.1 us
  Pallas kernels  62 us (94%)
  local copies, waits for them, and re-layouts  3.53 us (5%)
    pallas_call x1, Pallas kernels, per_device(): pl.pallas_call(functools.partial(kernel, n, m, n1, split, own * n * m), o...  62 us
    unnamed x4, local copies, waits for them, and re-layouts  3.53 us

profile of v2, /device:TPU:0, one launch (start us, length us, event | category | flops | bytes accessed | tf_op | source)
XLA Modules:
  0.0 66.1 jit_solution(16422310316130301962)
XLA Ops:
  0.6 62.0 %shard_map.41 = (f32[512,512]{1,0:T(8,128)}, f32[768,512]{1,0:T(8,128)}) custom-call(f32[384,512]{1,0:T(8,128)} %panel_ref.1, f32[768,512]{1,0:T(8,128)} %trailing_ref.1), custom_call_target="tpu_custom_call" | custom-call | tf_op jit(solution)/shard_map/pallas_call | solution.py:272
  62.6 0.0 copy-start
  62.6 2.4 %copy.6 = f32[512,512]{1,0:T(8,128)} copy(f32[512,512]{1,0:T(8,128)} %get-tuple-element.4) | data formatting | bytes 2097152
  65.0 0.0 copy-done
  65.0 1.1 %copy.7 = f32[768,512]{1,0:T(8,128)} copy(f32[768,512]{1,0:T(8,128)S(1)} %copy-done) | data formatting | bytes 3145728
Async XLA Ops:
  62.6 2.4 %copy-start = (f32[768,512]{1,0:T(8,128)S(1)}, f32[768,512]{1,0:T(8,128)}, u32[]{:S(2)}) copy-start(f32[768,512]{1,0:T(8,128)} %get-tuple-element.5) | copy-start | bytes 4718596
